TPU v7x, 128 devices: a whole 4x4x4 slice. The times are simulated.
128 devices in a mesh: comp: 2 (over z_hi), face: 4 (over z_lo, core), tile: 16 (over y, x).
Axes of the slice: x: 4, y: 4, z: 4 (z_hi: 2, z_lo: 2; z = z_hi * 2 + z_lo), core: 2. Of those that a mesh axis runs over, the one named last changes fastest.
Arguments:
- state: bfloat16 [2, 393216, 256], P('comp', ('face', 'tile')), may hold values from -6 to 6
- cycle_source: int32 [2, 22784], P('comp', ('face', 'tile')), may hold values from 0 to 4095
- halo_rows: int32 [2, 4, 65536], P('comp', None, ('face', 'tile')), may hold values from 0 to 6143
- halo_count: int32 [2, 4, 64], P('comp', None, ('face', 'tile')), may hold values from 256 to 1024, as said below
- couple_rows: int32 [2, 16, 8192], P('comp', None, ('face', 'tile')), may hold values from 0 to 6143, as said below
- couple_count: int32 [2, 16, 64], P('comp', None, ('face', 'tile')), may hold values from 32 to 128, as said below
- couple_land: int32 [2, 16, 8192], P('comp', None, ('face', 'tile')), may hold values from 0 to 6143, as said below
- couple_weight: bfloat16 [2, 256, 256], P('comp'), may hold values from -0.375 to 0.375
- dw_weight: float32 [2, 9, 256], P('comp'), may hold values from -2 to 2
- norm_gain: float32 [2, 256], P('comp'), may hold values from 0.25 to 1.75
- up_weight: bfloat16 [2, 256, 1024], P('comp'), may hold values from -0.375 to 0.375
- up_bias: float32 [2, 1024], P('comp'), may hold values from -3 to 3
- down_weight: bfloat16 [2, 1024, 256], P('comp'), may hold values from -0.1875 to 0.1875
Outputs:
- level_out: bfloat16 [2, 393216, 256], P('comp', ('face', 'tile'))
Inputs may be any that keep to these rules, and one draw needn't show every extreme that they name: `halo_count`: in each component and each direction some block sends exactly 1024 rows. `couple_count`: in every draw some block receives 128 rows from each of the 16 blocks of the other component in its face group. `couple_rows`: within one block the 2048 entries are distinct. `couple_land`: within one receiving block the 2048 entries are distinct.
All inputs are finite; a program needn't handle non-finite values.
Results may differ from a plain program's by a relative error of at most 0.0046.
Values may be sent and summed in bfloat16 or wider, within the bound.
A program may use at most 64 MiB of HBM per device.

v0:
```python
import jax
import jax.numpy as jnp
from jax import lax
from jax.sharding import PartitionSpec as P

GRID_W = 128


def from_behind(block, axis, distance):
    devices = range(lax.axis_size(axis))
    route = [((i - distance) % len(devices), i) for i in devices]
    return lax.ppermute(block, axis, route)


def tile_rim(pack_rows, offset):
    return from_behind(pack_rows, "tile", offset)


def face_rim(pack_rows, offset):
    return from_behind(pack_rows, "face", offset)


def body(
    state,
    cycle_source,
    halo_rows,
    halo_count,
    couple_rows,
    couple_count,
    couple_land,
    couple_weight,
    dw_weight,
    norm_gain,
    up_weight,
    up_bias,
    down_weight,
):
    own_rows = state[0]
    cell_count, channels = own_rows.shape
    tile_count = lax.axis_size("tile")
    slot_count = couple_rows.shape[2]
    picked = own_rows[couple_rows[0].reshape(-1)].reshape(tile_count, slot_count, channels)
    slot_iota = lax.broadcasted_iota(jnp.int32, (tile_count, slot_count, 1), 1)
    buckets = jnp.where(
        slot_iota < couple_count[0][:, :, None], picked, jnp.zeros((), jnp.bfloat16)
    )
    weight_pair = couple_weight[0]
    partner = 1 - lax.axis_index("comp")
    side_index = lax.broadcasted_iota(jnp.int32, (2, 1, 1, 1), 0)
    outgoing = jnp.where(side_index == partner, buckets[None], jnp.zeros((), jnp.bfloat16))
    outgoing = outgoing.reshape(2 * tile_count, slot_count, channels)
    incoming = lax.all_to_all(outgoing, ("comp", "tile"), split_axis=0, concat_axis=0, tiled=True)
    incoming = incoming.reshape(2, tile_count, slot_count, channels)
    arrived = jnp.einsum(
        "tsc,ce->tse",
        lax.dynamic_index_in_dim(incoming, partner, 0, keepdims=False),
        weight_pair,
        preferred_element_type=jnp.float32,
    )
    coupled = (
        jnp.zeros((cell_count, channels), jnp.float32)
        .at[couple_land[0].reshape(-1)]
        .set(arrived.reshape(-1, channels), unique_indices=True)
    )
    joined = (own_rows.astype(jnp.float32) + coupled).astype(jnp.bfloat16)
    rim_count = halo_rows.shape[2]
    rim_pick = joined[halo_rows[0].reshape(-1)].reshape(4, rim_count, channels)
    rim_iota = lax.broadcasted_iota(jnp.int32, (4, rim_count, 1), 1)
    packs = jnp.where(rim_iota < halo_count[0][:, :, None], rim_pick, jnp.zeros((), jnp.bfloat16))
    arrived_rims = jnp.concatenate(
        [
            tile_rim(packs[0], 1),
            tile_rim(packs[1], -1),
            face_rim(packs[2], 1),
            face_rim(packs[3], -1),
        ],
        0,
    )
    height = cell_count // GRID_W
    grid = joined.reshape(height, GRID_W, channels)
    border = arrived_rims[cycle_source[0]]
    top = border[: GRID_W + 2]
    bottom = border[GRID_W + 2 : 2 * GRID_W + 4]
    left = border[2 * GRID_W + 4 : 2 * GRID_W + 4 + height]
    right = border[2 * GRID_W + 4 + height :]
    middle = jnp.concatenate([left[:, None], grid, right[:, None]], 1)
    padded = jnp.concatenate([top[None], middle, bottom[None]], 0)
    dw_taps = dw_weight[0]
    mixed = jnp.zeros((height, GRID_W, channels), jnp.float32)
    for row_step in range(3):
        for col_step in range(3):
            window = padded[row_step : row_step + height, col_step : col_step + GRID_W]
            mixed = mixed + dw_taps[3 * row_step + col_step] * window.astype(jnp.float32)
    mixed = mixed.reshape(cell_count, channels)
    center = mixed - jnp.mean(mixed, axis=-1, keepdims=True)
    spread_sq = jnp.mean(center * center, axis=-1, keepdims=True)
    normed = (center * lax.rsqrt(spread_sq + 1e-06) * norm_gain[0]).astype(jnp.bfloat16)
    block_span = 2048
    block_total = cell_count // block_span
    w_up = up_weight[0]
    b_up = up_bias[0]
    w_down = down_weight[0]

    def one_block(inputs):
        block_normed, block_rows = inputs
        before = jnp.dot(block_normed, w_up, preferred_element_type=jnp.float32) + b_up
        hidden = jax.nn.gelu(before, approximate=True).astype(jnp.bfloat16)
        output = block_rows.astype(jnp.float32) + jnp.dot(
            hidden, w_down, preferred_element_type=jnp.float32
        )
        return output.astype(jnp.bfloat16)

    result = lax.map(
        one_block,
        (
            normed.reshape(block_total, block_span, channels),
            joined.reshape(block_total, block_span, channels),
        ),
    )
    return result.reshape(cell_count, channels)[None]


def solution(mesh):
    in_specs = (
        P("comp", ("face", "tile"), None),
        P("comp", ("face", "tile")),
        P("comp", None, ("face", "tile")),
        P("comp", None, ("face", "tile")),
        P("comp", None, ("face", "tile")),
        P("comp", None, ("face", "tile")),
        P("comp", None, ("face", "tile")),
        P("comp", None, None),
        P("comp", None, None),
        P("comp", None),
        P("comp", None, None),
        P("comp", None),
        P("comp", None, None),
    )
    out_specs = P("comp", ("face", "tile"), None)
    return jax.shard_map(body, mesh=mesh, in_specs=in_specs, out_specs=out_specs, check_vma=False)
```

profile of v0, /device:TPU:0, one launch (start us, length us, event | category | flops | bytes accessed | tf_op | source)
XLA Modules:
  0.0 157.5 jit_solution(14006545640499879609)
XLA Ops:
  0.0 0.1 broadcast_in_dim.81
  0.1 0.1 broadcast_in_dim.82
  0.2 0.7 compare_select_fusion.1
  0.9 0.7 iota_compare_fusion.1
  1.6 8.9 %gather_fusion = bf16[2048,256]{1,0:T(8,128)(2,1)S(1)} fusion(bf16[6144,256]{1,0:T(8,128)(2,1)} %bitcast.94, s32[2048]{0:T(1024)S(1)} %broadcast_clamp_fusion.1), kind=kCustom, calls=%fused_computation | custom fusion | bytes 2105344 | tf_op jit(solution)/shard_map/gather | solution.py:42
  10.6 0.4 broadcast_select_fusion.1
  11.1 1.5 bitcast_select_fusion
  12.6 10.7 %all-to-all-start = ((bf16[32,128,256]{2,1,0:T(8,128)(2,1)}), bf16[32,128,256]{2,1,0:T(8,128)(2,1)S(1)}, u32[]{:S(2)}, u32[]{:S(2)}) async-start(bf16[32,128,256]{2,1,0:T(8,128)(2,1)} %bitcast_select_fusion), calls=%async_computation | async-start | bytes 4194304 | tf_op jit(solution)/shard_map/all_to_all | solution.py:52
  23.4 0.1 iota_compare_fusion
  23.5 29.3 %all-to-all-done = bf16[32,128,256]{2,1,0:T(8,128)(2,1)S(1)} async-done(((bf16[32,128,256]{2,1,0:T(8,128)(2,1)}), bf16[32,128,256]{2,1,0:T(8,128)(2,1)S(1)}, u32[]{:S(2)}, u32[]{:S(2)}) %all-to-all-start) | async-done | bytes 2097184 | tf_op jit(solution)/shard_map/all_to_all | solution.py:52
  52.8 0.1 constant_dynamic-slice_fusion
  52.9 0.4 fusion.26
  53.3 12.1 %scatter_custom_fusion = f32[6144,256]{1,0:T(8,128)} fusion(s32[2048]{0:T(1024)S(1)} %bitcast.105, f32[2048,256]{1,0:T(8,128)S(1)} %fusion.26, f32[]{:T(128)} %constant.27.clone.1), kind=kCustom, calls=%fused_computation.35 | custom fusion | bytes 6291460 | tf_op jit(solution)/shard_map/scatter | solution.py:63
  65.4 4.4 %add_convert_fusion = bf16[6144,256]{1,0:T(8,128)(2,1)S(1)} fusion(f32[6144,256]{1,0:T(8,128)} %scatter_custom_fusion, bf16[1,6144,256]{2,1,0:T(8,128)(2,1)} %param.15), kind=kLoop, calls=%fused_computation.30 | loop fusion | flops 4718592 | bytes 12582912 | tf_op jit(solution)/shard_map/convert_element_type | solution.py:65
  69.8 17.0 %gather_fusion.1 = bf16[4096,256]{1,0:T(8,128)(2,1)} fusion(bf16[6144,256]{1,0:T(8,128)(2,1)S(1)} %add_convert_fusion, s32[4096]{0:T(1024)S(1)} %broadcast_clamp_fusion), kind=kCustom, calls=%fused_computation.1 | custom fusion | bytes 4210688 | tf_op jit(solution)/shard_map/gather | solution.py:67
  86.8 2.0 %broadcast_select_fusion = bf16[4,1024,256]{2,1,0:T(8,128)(2,1)S(1)} fusion(bf16[4,1024,256]{2,1,0:T(8,128)(2,1)} %bitcast.95, pred[4,1024]{1,0:T(4,128)(4,1)S(1)} %iota_compare_fusion), kind=kLoop, calls=%fused_computation.39 | loop fusion | flops 1048576 | bytes 4198400 | tf_op jit(solution)/shard_map/jit(_where)/select_n | solution.py:69
  88.8 1.4 slice_bitcast_fusion.3
  90.2 1.3 collective-permute-start
  91.5 4.0 %collective-permute-start.1 = (bf16[1024,256]{1,0:T(8,128)(2,1)}, bf16[1024,256]{1,0:T(8,128)(2,1)}, u32[]{:S(2)}, u32[]{:S(2)}) collective-permute-start(bf16[1024,256]{1,0:T(8,128)(2,1)} %get-tuple-element.64), channel_id=1, source_target_pairs={{1,0},{2,1},{3,2},{4,3},{5,4},{6,5},{7,6},{8,7},{9,8},{10,9},{11,1... | collective-permute-start | bytes 1572872 | tf_op jit(solution)/shard_map/ppermute | solution.py:12
  95.5 1.7 %collective-permute-start.3 = (bf16[1024,256]{1,0:T(8,128)(2,1)}, bf16[1024,256]{1,0:T(8,128)(2,1)}, u32[]{:S(2)}, u32[]{:S(2)}) collective-permute-start(bf16[1024,256]{1,0:T(8,128)(2,1)} %get-tuple-element.62), channel_id=1, source_target_pairs={{16,0},{32,16},{48,32},{0,48},{17,1},{33,17},{49,33},{1,49},{18,2}... | collective-permute-start | bytes 1572872 | tf_op jit(solution)/shard_map/ppermute | solution.py:12
  97.3 8.8 %collective-permute-done = bf16[1024,256]{1,0:T(8,128)(2,1)} collective-permute-done((bf16[1024,256]{1,0:T(8,128)(2,1)}, bf16[1024,256]{1,0:T(8,128)(2,1)}, u32[]{:S(2)}, u32[]{:S(2)}) %collective-permute-start) | collective-permute-done | bytes 524320 | tf_op jit(solution)/shard_map/ppermute | solution.py:12
  106.1 2.6 %collective-permute-done.2 = bf16[1024,256]{1,0:T(8,128)(2,1)} collective-permute-done((bf16[1024,256]{1,0:T(8,128)(2,1)}, bf16[1024,256]{1,0:T(8,128)(2,1)}, u32[]{:S(2)}, u32[]{:S(2)}) %collective-permute-start.2) | collective-permute-done | bytes 524320 | tf_op jit(solution)/shard_map/ppermute | solution.py:12
  108.7 3.0 %pad_maximum_fusion.3 = bf16[4096,256]{1,0:T(8,128)(2,1)} fusion(bf16[1024,256]{1,0:T(8,128)(2,1)} %collective-permute-done.3, bf16[1024,256]{1,0:T(8,128)(2,1)} %collective-permute-done.2, bf16[1024,256]{1,0:T(8,128)(2,1)} %collective-permute-done.1, bf16[1024,256]{1,0:T(8,128)(2,1)} %collective-permute-done), kind=kLoop, calls=%fused_computation.37 | loop fusion | flops 8388608 | bytes 4194304 | tf_op jit(solution)/shard_map/concatenate | solution.py:70
  111.7 3.5 %gather_fusion.2 = bf16[356,256]{1,0:T(8,128)(2,1)S(1)} fusion(bf16[4096,256]{1,0:T(8,128)(2,1)} %pad_maximum_fusion.3, s32[1024]{0:T(1024)S(1)} %pad_clamp_fusion), kind=kCustom, calls=%fused_computation.2 | custom fusion | bytes 365968 | tf_op jit(solution)/shard_map/gather | solution.py:81
  115.4 5.4 %maximum_maximum_fusion = (bf16[49,130,256]{2,1,0:T(8,128)(2,1)S(1)}, bf16[49,130,256]{2,1,0:T(8,128)(2,1)S(1)}) fusion(bf16[48,1,256]{2,1,0:T(2,128)(2,1)S(1)} %copy.19, bf16[48,128,256]{2,1,0:T(8,128)(2,1)S(1)} %bitcast.90, bf16[48,1,256]{2,1,0:T(2,128)(2,1)S(1)} %copy.18, bf16[1,130,256]{2,1,0:T(8,128)(2,1)S(1)} %get-tuple-element.65, ...), kind=kLoop, calls=%fused_computation.31 | loop fusion | flops 26091520 | bytes 9850880 | tf_op jit(solution)/shard_map/concatenate | solution.py:87
  120.8 8.8 %fusion.29 = (f32[48,128]{1,0:T(8,128)S(1)}, f32[48,128,256]{2,1,0:T(8,128)}) fusion(bf16[49,130,256]{2,1,0:T(8,128)(2,1)S(1)} %get-tuple-element.60, f32[256]{0:T(256)S(1)} %bitcast.113, f32[256]{0:T(256)S(1)} %bitcast.114, f32[256]{0:T(256)S(1)} %bitcast.107, bf16[48,1,256]{2,1,0:T(2,128)(2,1)S(1)} %copy.19, bf16[48,128,256]{2,1,0:T(8,128)(2,1)S(1)} %bitcast.91, ...), kind=kLoop, calls=%fused_computation.65 | loop fusion | flops 51898368 | bytes 28394496 | tf_op jit(solution)/shard_map/reduce_sum | solution.py:95
  129.6 3.8 %multiply_reduce_fusion = f32[48,128]{1,0:T(8,128)S(1)} fusion(f32[48,128,256]{2,1,0:T(8,128)} %get-tuple-element.58, f32[48,128]{1,0:T(8,128)S(1)} %broadcast_multiply_fusion), kind=kLoop, calls=%fused_computation.28 | loop fusion | flops 4712448 | bytes 6340608 | tf_op jit(solution)/shard_map/reduce_sum | solution.py:96
  133.5 6.3 %fusion.23 = bf16[3,2048,256]{2,1,0:T(8,128)(2,1)} fusion(f32[256]{0:T(256)S(1)} %bitcast.115, f32[3,2048]{1,0:T(4,128)S(1)} %rsqrt.12, f32[3,2048]{1,0:T(4,128)S(1)} %div.9, f32[3,2048,256]{2,1,0:T(8,128)} %bitcast.93), kind=kLoop, calls=%fused_computation.27 | loop fusion | flops 6291456 | bytes 9487360 | tf_op jit(solution)/shard_map/convert_element_type | solution.py:97
  139.7 17.7 %while.10 = (s32[]{:T(128)}, bf16[3,2048,256]{2,1,0:T(8,128)(2,1)}, bf16[3,2048,256]{2,1,0:T(8,128)(2,1)S(1)}, bf16[3,2048,256]{2,1,0:T(8,128)(2,1)}, bf16[256,1...) while((s32[]{:T(128)}, bf16[3,2048,256]{2,1,0:T(8,128)(2,1)}, ...), condition=%wide.region_4.5_spmd, body=%wide.region_3.4_spmd.sunk | while | flops 2170028032 | bytes 4199509 | solution.py:113
  139.7 5.9 %fusion.41 = bf16[3,2048,256]{2,1,0:T(8,128)(2,1)} fusion(bf16[3,2048,256]{2,1,0:T(8,128)(2,1)} %get-tuple-element.130, s32[]{:T(128)} %get-tuple-element.129, bf16[1024,256]{1,0:T(8,128)(2,1)} %get-tuple-element.143, bf16[256,1024]{1,0:T(8,128)(2,1)} %get-tuple-element.141, f32[1024]{0:T(1024)S(1)} %bitcast.120, ...), kind=kOutput, calls=%fused_computation.16.clone.1 | convolution fusion | flops 2170028032 | bytes 4199424 | tf_op jit(solution)/shard_map/while/body/eval_jaxpr/dot_general | solution.py:108
  145.6 5.9 %fusion.41 = bf16[3,2048,256]{2,1,0:T(8,128)(2,1)} fusion(bf16[3,2048,256]{2,1,0:T(8,128)(2,1)} %get-tuple-element.130, s32[]{:T(128)} %get-tuple-element.129, bf16[1024,256]{1,0:T(8,128)(2,1)} %get-tuple-element.143, bf16[256,1024]{1,0:T(8,128)(2,1)} %get-tuple-element.141, f32[1024]{0:T(1024)S(1)} %bitcast.120, ...), kind=kOutput, calls=%fused_computation.16.clone.1 | convolution fusion | flops 2170028032 | bytes 4199424 | tf_op jit(solution)/shard_map/while/body/eval_jaxpr/dot_general | solution.py:108
  151.5 5.9 %fusion.41 = bf16[3,2048,256]{2,1,0:T(8,128)(2,1)} fusion(bf16[3,2048,256]{2,1,0:T(8,128)(2,1)} %get-tuple-element.130, s32[]{:T(128)} %get-tuple-element.129, bf16[1024,256]{1,0:T(8,128)(2,1)} %get-tuple-element.143, bf16[256,1024]{1,0:T(8,128)(2,1)} %get-tuple-element.141, f32[1024]{0:T(1024)S(1)} %bitcast.120, ...), kind=kOutput, calls=%fused_computation.16.clone.1 | convolution fusion | flops 2170028032 | bytes 4199424 | tf_op jit(solution)/shard_map/while/body/eval_jaxpr/dot_general | solution.py:108
  (37 shorter events, 0.3 us)
Async XLA Ops:
  0.0 52.9 %copy-start = (bf16[1,256,256]{2,1,0:T(8,128)(2,1)S(1)}, bf16[1,256,256]{2,1,0:T(8,128)(2,1)}, u32[]{:S(2)}) copy-start(bf16[1,256,256]{2,1,0:T(8,128)(2,1)} %param.22) | copy-start | bytes 393220
  10.6 12.7 %copy-start.1 = (s32[1,4,1024]{2,1,0:T(4,128)S(1)}, s32[1,4,1024]{2,1,0:T(4,128)}, u32[]{:S(2)}) copy-start(s32[1,4,1024]{2,1,0:T(4,128)} %param.17) | copy-start | bytes 49156
  10.6 12.8 %copy-start.6 = (s32[1,4,1]{1,2,0:T(1,128)S(1)}, s32[1,4,1]{1,2,0:T(1,128)}, u32[]{:S(2)}) copy-start(s32[1,4,1]{1,2,0:T(1,128)} %param.18) | copy-start | bytes 52
  10.6 12.9 %copy-start.3 = (s32[1,16,128]{2,1,0:T(8,128)S(1)}, s32[1,16,128]{2,1,0:T(8,128)}, u32[]{:S(2)}) copy-start(s32[1,16,128]{2,1,0:T(8,128)} %param.21) | copy-start | bytes 24580
  12.6 40.2 %all-to-all-start = ((bf16[32,128,256]{2,1,0:T(8,128)(2,1)}), bf16[32,128,256]{2,1,0:T(8,128)(2,1)S(1)}, u32[]{:S(2)}, u32[]{:S(2)}) async-start(bf16[32,128,256]{2,1,0:T(8,128)(2,1)} %bitcast_select_fusion), calls=%async_computation | async-start | bytes 4194304 | tf_op jit(solution)/shard_map/all_to_all | solution.py:52
  86.8 10.5 %copy-start.4 = (s32[1,356]{1,0:T(1,128)S(1)}, s32[1,356]{1,0:T(1,128)}, u32[]{:S(2)}) copy-start(s32[1,356]{1,0:T(1,128)} %param.16) | copy-start | bytes 4276
  86.8 10.5 %copy-start.2 = (f32[1,9,256]{2,0,1:T(1,128)S(1)}, f32[1,9,256]{2,0,1:T(1,128)}, u32[]{:S(2)}) copy-start(f32[1,9,256]{2,0,1:T(1,128)} %param.23) | copy-start | bytes 27652
  90.2 16.0 %collective-permute-start = (bf16[1024,256]{1,0:T(8,128)(2,1)}, bf16[1024,256]{1,0:T(8,128)(2,1)}, u32[]{:S(2)}, u32[]{:S(2)}) collective-permute-start(bf16[1024,256]{1,0:T(8,128)(2,1)} %get-tuple-element.61), channel_id=1, source_target_pairs={{15,0},{0,1},{1,2},{2,3},{3,4},{4,5},{5,6},{6,7},{7,8},{8,9},{9,10... | collective-permute-start | bytes 1572872 | tf_op jit(solution)/shard_map/ppermute | solution.py:12
  91.5 14.6 %collective-permute-start.1 = (bf16[1024,256]{1,0:T(8,128)(2,1)}, bf16[1024,256]{1,0:T(8,128)(2,1)}, u32[]{:S(2)}, u32[]{:S(2)}) collective-permute-start(bf16[1024,256]{1,0:T(8,128)(2,1)} %get-tuple-element.64), channel_id=1, source_target_pairs={{1,0},{2,1},{3,2},{4,3},{5,4},{6,5},{7,6},{8,7},{9,8},{10,9},{11,1... | collective-permute-start | bytes 1572872 | tf_op jit(solution)/shard_map/ppermute | solution.py:12
  95.5 13.2 %collective-permute-start.2 = (bf16[1024,256]{1,0:T(8,128)(2,1)}, bf16[1024,256]{1,0:T(8,128)(2,1)}, u32[]{:S(2)}, u32[]{:S(2)}) collective-permute-start(bf16[1024,256]{1,0:T(8,128)(2,1)} %get-tuple-element.63), channel_id=1, source_target_pairs={{48,0},{0,16},{16,32},{32,48},{49,1},{1,17},{17,33},{33,49},{50,2}... | collective-permute-start | bytes 1572872 | tf_op jit(solution)/shard_map/ppermute | solution.py:12
  95.5 13.2 %collective-permute-start.3 = (bf16[1024,256]{1,0:T(8,128)(2,1)}, bf16[1024,256]{1,0:T(8,128)(2,1)}, u32[]{:S(2)}, u32[]{:S(2)}) collective-permute-start(bf16[1024,256]{1,0:T(8,128)(2,1)} %get-tuple-element.62), channel_id=1, source_target_pairs={{16,0},{32,16},{48,32},{0,48},{17,1},{33,17},{49,33},{1,49},{18,2}... | collective-permute-start | bytes 1572872 | tf_op jit(solution)/shard_map/ppermute | solution.py:12
  129.6 3.8 %copy-start.5 = (f32[1,256]{1,0:T(1,128)S(1)}, f32[1,256]{1,0:T(1,128)}, u32[]{:S(2)}) copy-start(f32[1,256]{1,0:T(1,128)} %param.24) | copy-start | bytes 3076
  133.4 6.3 %copy-start.7 = (f32[1,1024]{1,0:T(1,128)S(1)}, f32[1,1024]{1,0:T(1,128)}, u32[]{:S(2)}) copy-start(f32[1,1024]{1,0:T(1,128)} %param.26) | copy-start | bytes 12292
where the time goes:
time: 160 us; the launch traced here: 157 us
  local copies, waits for them, and re-layouts  43.4 us (27%)
  waiting for transfers between devices  40.7 us (25%)
  other arithmetic  37.2 us (23%)
  matrix products  18.2 us (11%)
  starting transfers between devices  17.8 us (11%)
    all_to_all x1, waiting for transfers between devices, body(): lax.all_to_all(outgoing, ('comp', 'tile'), split_axis=0, concat_axis=0, t...  29.3 us
    dot_general x3, matrix products, one_block(): jnp.dot(hidden, w_down, preferred_element_type=jnp.float32)  17.7 us
    gather x1, local copies, waits for them, and re-layouts, body(): rim_pick = joined[halo_rows[0].reshape(-1)].reshape(4, rim_count, channels)  17 us
    scatter x1, local copies, waits for them, and re-layouts, body(): coupled = jnp.zeros((cell_count, channels), jnp.float32).at[couple_land[0...  12.1 us
    ppermute x4, waiting for transfers between devices, from_behind(): return lax.ppermute(block, axis, route)  11.4 us
    all_to_all x1, starting transfers between devices, body(): lax.all_to_all(outgoing, ('comp', 'tile'), split_axis=0, concat_axis=0, t...  10.7 us
    gather x1, local copies, waits for them, and re-layouts, body(): own_rows[couple_rows[0].reshape(-1)]  8.93 us
    reduce_sum x1, other arithmetic, body(): center = mixed - jnp.mean(mixed, axis=-1, keepdims=True)  8.79 us
  transfers between devices with their start and end apart: 5, of which 3 were waited for; matrix products, arithmetic and copies ran while one was open for 0% of the time, Pallas kernels for 0%

commit v1 on v0

v1 whole, which is shorter than its diff:
```python
import functools

import jax
import jax.numpy as jnp
from jax import lax
from jax.experimental import pallas as pl
from jax.experimental.pallas import tpu as pltpu
from jax.sharding import PartitionSpec as P

MESH = pl.DeviceIdType.MESH
GRID_W = 128
F32 = jnp.float32
BF16 = jnp.bfloat16


def place(comp, face, tile):
    return {"comp": comp, "face": face, "tile": tile}


def couple_kernel(
    tiles,
    faces,
    cycle_len,
    border_rows,
    state_ref,
    cycle_ref,
    halo_rows_ref,
    halo_count_ref,
    couple_rows_ref,
    couple_count_ref,
    couple_land_ref,
    couple_weight_ref,
    dw_ref,
    gain_ref,
    joined_out,
    normed_out,
    rows_bf,
    rows_f32,
    picked,
    send_rows,
    recv_rows,
    cycle_near,
    cycle_smem,
    halo_index,
    halo_send,
    halo_recv,
    border,
    columns,
    edge,
    normed,
    load_sem,
    smem_sem,
    store_sem,
    couple_send_sem,
    couple_recv_sem,
    cycle_send_sem,
    cycle_recv_sem,
    halo_send_sem,
    halo_recv_sem,
):
    comp, face, tile = lax.axis_index("comp"), lax.axis_index("face"), lax.axis_index("tile")
    cells, channels = rows_bf.shape
    height = cells // GRID_W
    slots = couple_rows_ref.shape[2]
    rim_rows = halo_rows_ref.shape[2]
    other = 1 - comp
    near = [
        place(comp, face, lax.rem(tile + 1, tiles)),
        place(comp, face, lax.rem(tile + tiles - 1, tiles)),
        place(comp, lax.rem(face + 1, faces), tile),
        place(comp, lax.rem(face + faces - 1, faces), tile),
    ]

    load_chunks = 4
    chunk = cells // load_chunks

    def load(k):
        part = pl.ds(k * chunk, chunk)
        return pltpu.make_async_copy(state_ref.at[0, part], rows_bf.at[part], load_sem.at[k])

    for k in range(load_chunks):
        load(k).start()

    barrier = pltpu.get_barrier_semaphore()

    def greet(k, carry):
        pl.semaphore_signal(barrier, inc=1, device_id=place(other, face, k), device_id_type=MESH)
        return carry

    lax.fori_loop(0, tiles, greet, 0)
    for target in near:
        pl.semaphore_signal(barrier, inc=1, device_id=target, device_id_type=MESH)

    rows_f32[pl.ds(cells, 8), :] = jnp.zeros((8, channels), F32)
    for k in range(load_chunks):
        load(k).wait()

        def widen(i, carry, k=k):
            part = pl.ds(pl.multiple_of(k * chunk + i * 128, 128), 128)
            rows_f32[part, :] = rows_bf[part, :].astype(F32)
            return carry

        lax.fori_loop(0, chunk // 128, widen, 0)

    pl.semaphore_wait(barrier, tiles + 4)

    def cycle_copy(d):
        return pltpu.make_async_remote_copy(
            src_ref=cycle_ref,
            dst_ref=cycle_near.at[d],
            send_sem=cycle_send_sem.at[d],
            recv_sem=cycle_recv_sem.at[d],
            device_id=near[d ^ 1],
            device_id_type=MESH,
        )

    for d in range(4):
        cycle_copy(d).start()

    def couple_copy(k):
        part = pl.ds(pl.multiple_of(k * slots, slots), slots)
        return pltpu.make_async_remote_copy(
            src_ref=send_rows.at[part],
            dst_ref=recv_rows.at[part],
            send_sem=couple_send_sem.at[k],
            recv_sem=couple_recv_sem.at[k],
            device_id=place(other, face, lax.rem(tile + k, tiles)),
            device_id_type=MESH,
        )

    def gather_send(k, carry):
        dest = lax.rem(tile + k, tiles)
        live = couple_count_ref[0, dest, 0]

        def pick(g, inner):
            for u in range(8):
                s = g * 8 + u
                index = jnp.where(s < live, couple_rows_ref[0, dest, s], cells)
                picked[pl.ds(s, 1), :] = rows_f32[pl.ds(index, 1), :]
            return inner

        lax.fori_loop(0, slots // 8, pick, 0)
        part = pl.ds(pl.multiple_of(k * slots, slots), slots)
        send_rows[part, :] = picked[pl.ds(0, slots), :].astype(BF16)
        couple_copy(k).start()
        return carry

    lax.fori_loop(0, tiles, gather_send, 0)

    for d in range(4):
        cycle_copy(d).wait()
    to_smem = pltpu.make_async_copy(cycle_near, cycle_smem, smem_sem)
    to_smem.start()
    to_smem.wait()
    for d in range(4):
        live = halo_count_ref[0, d, 0]

        def resolve(g, carry, d=d, live=live):
            for u in range(4):
                r = g * 4 + u
                asked = cycle_smem[d, 0, r]
                s = jnp.bitwise_and(asked, rim_rows - 1)
                mine = (asked >= d * rim_rows) & (asked < (d + 1) * rim_rows) & (s < live)
                halo_index[d, r] = jnp.where(mine, halo_rows_ref[0, d, s], cells)
            return carry

        lax.fori_loop(0, cycle_len // 4, resolve, 0)

        def unasked(r, carry, d=d):
            halo_index[d, r] = cells
            return carry

        lax.fori_loop(cycle_len, border_rows, unasked, 0)

    pair = 2 * slots
    span = 4
    lane_col = lax.broadcasted_iota(jnp.int32, (GRID_W, pair), 0)

    def land_pair(p, last):
        part = pl.ds(pl.multiple_of(p * pair, pair), pair)
        rows = recv_rows[part, :]
        arrived = jnp.dot(rows, couple_weight_ref[0], preferred_element_type=F32)
        high = arrived.astype(BF16)
        low = (arrived - high.astype(F32)).astype(BF16)
        land = jnp.concatenate(
            [
                couple_land_ref[0, pl.ds(lax.rem(tile - (2 * p + q) + tiles, tiles), 1), :]
                for q in range(2)
            ],
            axis=1,
        )
        land_row = jnp.right_shift(land, 7)
        in_col = jnp.where(jnp.bitwise_and(land, GRID_W - 1) == lane_col, 1.0, 0.0).astype(BF16)

        def block(b, carry):
            hot = jnp.concatenate(
                [
                    in_col * jnp.where(land_row == b * span + q, 1.0, 0.0).astype(BF16)
                    for q in range(span)
                ],
                axis=0,
            )
            where = pl.ds(pl.multiple_of(b * span * GRID_W, span * GRID_W), span * GRID_W)
            added = jnp.dot(hot, high, preferred_element_type=F32)
            added = added + jnp.dot(hot, low, preferred_element_type=F32)
            total = rows_f32[where, :] + added
            if last:
                rounded = total.astype(BF16)
                rows_bf[where, :] = rounded
                total = rounded.astype(F32)
            rows_f32[where, :] = total
            return carry

        lax.fori_loop(0, height // span, block, 0)

    def land_step(p, carry):
        couple_copy(2 * p).wait_recv()
        couple_copy(2 * p + 1).wait_recv()
        land_pair(p, False)
        return carry

    lax.fori_loop(0, tiles // 2 - 1, land_step, 0)
    couple_copy(tiles - 2).wait_recv()
    couple_copy(tiles - 1).wait_recv()
    land_pair(tiles // 2 - 1, True)

    joined_store = pltpu.make_async_copy(rows_bf, joined_out, store_sem.at[0])
    joined_store.start()

    def halo_copy(d):
        return pltpu.make_async_remote_copy(
            src_ref=halo_send.at[d],
            dst_ref=halo_recv.at[d],
            send_sem=halo_send_sem.at[d],
            recv_sem=halo_recv_sem.at[d],
            device_id=near[d],
            device_id_type=MESH,
        )

    for d in (2, 3, 0, 1):

        def pick_halo(g, carry, d=d):
            for u in range(8):
                r = g * 8 + u
                picked[pl.ds(r, 1), :] = rows_f32[pl.ds(halo_index[d, r], 1), :]
            return carry

        lax.fori_loop(0, border_rows // 8, pick_halo, 0)
        halo_send[d] = picked[...].astype(BF16)
        halo_copy(d).start()

    taps = dw_ref[0]
    gain = gain_ref[0:1, :]

    def norm(mixed):
        center = mixed - jnp.mean(mixed, axis=-1, keepdims=True)
        spread = jnp.mean(center * center, axis=-1, keepdims=True)
        return center * lax.rsqrt(spread + 1e-06) * gain

    def mix(above, here, below):
        left, mid, right = (
            taps[c : c + 1] * above + taps[3 + c : 4 + c] * here + taps[6 + c : 7 + c] * below
            for c in range(3)
        )
        return mid + pltpu.roll(left, 1, 0) + pltpu.roll(right, GRID_W - 1, 0)

    def grid_row(i):
        return rows_f32[pl.ds(pl.multiple_of(i * GRID_W, GRID_W), GRID_W), :]

    def interior(i, carry):
        mixed = mix(grid_row(i - 1), grid_row(i), grid_row(i + 1))
        normed[pl.ds(pl.multiple_of(i * GRID_W, GRID_W), GRID_W), :] = norm(mixed).astype(BF16)
        return carry

    lax.fori_loop(1, height - 1, interior, 0)

    for d in range(4):
        halo_copy(d).wait_recv()
    border[...] = (halo_recv[0].astype(F32) + halo_recv[1].astype(F32)) + (
        halo_recv[2].astype(F32) + halo_recv[3].astype(F32)
    )
    wide = GRID_W + 2
    normed[pl.ds(0, GRID_W), :] = norm(
        mix(border[pl.ds(1, GRID_W), :], grid_row(0), grid_row(1))
    ).astype(BF16)
    normed[pl.ds(cells - GRID_W, GRID_W), :] = norm(
        mix(grid_row(height - 2), grid_row(height - 1), border[pl.ds(wide + 1, GRID_W), :])
    ).astype(BF16)

    outer = ((1, 0), (2, 1), (3, GRID_W - 2), (4, GRID_W - 1))

    def take_columns(i, carry):
        for q, col in outer:
            columns[q, pl.ds(i + 1, 1), :] = rows_f32[pl.ds(i * GRID_W + col, 1), :]
        return carry

    lax.fori_loop(0, height, take_columns, 0)
    for q, col in outer:
        columns[q, pl.ds(0, 1), :] = border[pl.ds(1 + col, 1), :]
        columns[q, pl.ds(height + 1, 1), :] = border[pl.ds(wide + 1 + col, 1), :]
    for q, corner, side in ((0, 0, 2 * wide), (5, wide - 1, 2 * wide + height)):
        columns[q, pl.ds(0, 1), :] = border[pl.ds(corner, 1), :]
        columns[q, pl.ds(1, height), :] = border[pl.ds(side, height), :]
        columns[q, pl.ds(height + 1, 1), :] = border[pl.ds(wide + corner, 1), :]
    for e, first in ((0, 0), (1, 3)):
        mixed = jnp.zeros((height, channels), F32)
        for r in range(3):
            for c in range(3):
                mixed = mixed + taps[3 * r + c : 3 * r + c + 1] * columns[first + c, pl.ds(r, height), :]
        edge[e] = norm(mixed)
    tile_rows = 16
    tile_iota = lax.broadcasted_iota(jnp.int32, (tile_rows, channels), 0)

    def merge(i, carry):
        for e, start, line in ((0, 0, 0), (1, GRID_W - tile_rows, tile_rows - 1)):
            part = pl.ds(pl.multiple_of(i * GRID_W + start, tile_rows), tile_rows)
            fixed = jnp.where(tile_iota == line, edge[e, pl.ds(i, 1), :], normed[part, :].astype(F32))
            normed[part, :] = fixed.astype(BF16)
        return carry

    lax.fori_loop(0, height, merge, 0)
    normed_store = pltpu.make_async_copy(normed, normed_out, store_sem.at[1])
    normed_store.start()
    for k in range(tiles):
        couple_copy(k).wait_send()
    for d in range(4):
        halo_copy(d).wait_send()
    joined_store.wait()
    normed_store.wait()


def mlp_kernel(normed_ref, joined_ref, up_ref, bias_ref, down_ref, out_ref):
    normed = normed_ref[...]
    width = up_ref.shape[2]
    total = joined_ref[...].astype(F32)
    step = 256
    for h in range(0, width, step):
        v = jnp.dot(normed, up_ref[0, :, h : h + step], preferred_element_type=F32)
        v = v + bias_ref[0:1, h : h + step]
        inner = v * (0.7978845608028654 + 0.035677408136300125 * (v * v))
        half = 0.5 * v
        hidden = (half + half * jnp.tanh(inner)).astype(BF16)
        total = total + jnp.dot(hidden, down_ref[0, h : h + step, :], preferred_element_type=F32)
    out_ref[0] = total.astype(BF16)


def body(
    state,
    cycle_source,
    halo_rows,
    halo_count,
    couple_rows,
    couple_count,
    couple_land,
    couple_weight,
    dw_weight,
    norm_gain,
    up_weight,
    up_bias,
    down_weight,
):
    _, cells, channels = state.shape
    tiles, faces = lax.axis_size("tile"), lax.axis_size("face")
    cycle_len = cycle_source.shape[1]
    border_rows = -(-cycle_len // 16) * 16
    slots = couple_rows.shape[2]
    height = cells // GRID_W
    vmem = pl.BlockSpec(memory_space=pltpu.VMEM)
    smem = pl.BlockSpec(memory_space=pltpu.SMEM)
    hbm = pl.BlockSpec(memory_space=pl.ANY)
    dma = pltpu.SemaphoreType.DMA
    joined, normed = pl.pallas_call(
        functools.partial(couple_kernel, tiles, faces, cycle_len, border_rows),
        name="couple_and_mix",
        out_shape=[jax.ShapeDtypeStruct((cells, channels), BF16)] * 2,
        in_specs=[hbm, vmem, smem, smem, smem, smem, vmem, vmem, vmem, vmem],
        out_specs=[hbm, hbm],
        scratch_shapes=[
            pltpu.VMEM((cells, channels), BF16),
            pltpu.VMEM((cells + 8, channels), F32),
            pltpu.VMEM((border_rows, channels), F32),
            pltpu.VMEM((tiles * slots, channels), BF16),
            pltpu.VMEM((tiles * slots, channels), BF16),
            pltpu.VMEM((4, 1, cycle_len), jnp.int32),
            pltpu.SMEM((4, 1, cycle_len), jnp.int32),
            pltpu.SMEM((4, border_rows), jnp.int32),
            pltpu.VMEM((4, border_rows, channels), BF16),
            pltpu.VMEM((4, border_rows, channels), BF16),
            pltpu.VMEM((border_rows, channels), F32),
            pltpu.VMEM((6, height + 8, channels), F32),
            pltpu.VMEM((2, height, channels), F32),
            pltpu.VMEM((cells, channels), BF16),
            dma((4,)),
            dma,
            dma((2,)),
            dma((tiles,)),
            dma((tiles,)),
            dma((4,)),
            dma((4,)),
            dma((4,)),
            dma((4,)),
        ],
        compiler_params=pltpu.CompilerParams(
            collective_id=0, has_side_effects=True, vmem_limit_bytes=40 << 20
        ),
    )(
        state,
        cycle_source,
        halo_rows,
        halo_count,
        couple_rows,
        couple_count,
        couple_land,
        couple_weight,
        dw_weight,
        norm_gain,
    )
    rows = 1024
    width = up_weight.shape[2]
    return pl.pallas_call(
        mlp_kernel,
        name="mlp",
        grid=(cells // rows,),
        out_shape=jax.ShapeDtypeStruct((1, cells, channels), BF16),
        in_specs=[
            pl.BlockSpec((rows, channels), lambda i: (i, 0)),
            pl.BlockSpec((rows, channels), lambda i: (i, 0)),
            pl.BlockSpec((1, channels, width), lambda i: (0, 0, 0)),
            pl.BlockSpec((1, width), lambda i: (0, 0)),
            pl.BlockSpec((1, width, channels), lambda i: (0, 0, 0)),
        ],
        out_specs=pl.BlockSpec((1, rows, channels), lambda i: (0, i, 0)),
        compiler_params=pltpu.CompilerParams(vmem_limit_bytes=40 << 20),
        cost_estimate=pl.CostEstimate(
            flops=4 * cells * channels * width, bytes_accessed=6 * cells * channels, transcendentals=cells * width
        ),
    )(normed, joined, up_weight, up_bias, down_weight)


def solution(mesh):
    in_specs = (
        P("comp", ("face", "tile"), None),
        P("comp", ("face", "tile")),
        P("comp", None, ("face", "tile")),
        P("comp", None, ("face", "tile")),
        P("comp", None, ("face", "tile")),
        P("comp", None, ("face", "tile")),
        P("comp", None, ("face", "tile")),
        P("comp", None, None),
        P("comp", None, None),
        P("comp", None),
        P("comp", None, None),
        P("comp", None),
        P("comp", None, None),
    )
    out_specs = P("comp", ("face", "tile"), None)
    return jax.shard_map(body, mesh=mesh, in_specs=in_specs, out_specs=out_specs, check_vma=False)
```

time: 160 us -> 106 us (0.66); the launches traced: 157 us -> 105 us
  Pallas kernels: 0 us -> 96.9 us
  waiting for transfers between devices: 40.7 us -> 0 us
  other arithmetic: 37.2 us -> 0 us
  local copies, waits for them, and re-layouts: 43.4 us -> 8.46 us
  matrix products: 18.2 us -> 0 us
  starting transfers between devices: 17.8 us -> 0 us
    pallas_call x0 -> x2, Pallas kernels: none -> 96.9 us  [the longest x1 86 us: body(): pl.pallas_call(functools.partial(couple_kernel, tiles, faces, cycle_len,...]
    gather x3 -> x0, local copies, waits for them, and re-layouts: 29.5 us -> none  [the longest x1 17 us: body(): rim_pick = joined[halo_rows[0].reshape(-1)].reshape(4, rim_count, channels)]
    all_to_all x1 -> x0, waiting for transfers between devices: 29.3 us -> none  [body(): lax.all_to_all(outgoing, ('comp', 'tile'), split_axis=0, concat_axis=0, t...]
    dot_general x4 -> x0, matrix products: 18.2 us -> none  [the longest x3 17.7 us: one_block(): jnp.dot(hidden, w_down, preferred_element_type=jnp.float32)]
    reduce_sum x2 -> x0, other arithmetic: 12.5 us -> none  [the longest x1 8.79 us: body(): center = mixed - jnp.mean(mixed, axis=-1, keepdims=True)]
    scatter x1 -> x0, local copies, waits for them, and re-layouts: 12.1 us -> none  [body(): coupled = jnp.zeros((cell_count, channels), jnp.float32).at[couple_land[0...]
    ppermute x4 -> x0, waiting for transfers between devices: 11.4 us -> none  [from_behind(): return lax.ppermute(block, axis, route)]
    all_to_all x1 -> x0, starting transfers between devices: 10.7 us -> none  [body(): lax.all_to_all(outgoing, ('comp', 'tile'), split_axis=0, concat_axis=0, t...]
  transfers between devices with their start and end apart: 5 -> 0, of which waited for: 3 -> 0; matrix products, arithmetic and copies ran while one was open for 0% -> 0% of each run, Pallas kernels for 0% -> 0%
where the time goes in v1:
time: 106 us; the launch traced here: 105 us
  Pallas kernels  96.9 us (91%)
  local copies, waits for them, and re-layouts  8.46 us (8%)
    pallas_call x1, Pallas kernels, body(): pl.pallas_call(functools.partial(couple_kernel, tiles, faces, cycle_len,...  86 us
    pallas_call x1, Pallas kernels, body(): pl.pallas_call(mlp_kernel, name='mlp', grid=(cells // rows,), out_shape=j...  10.9 us
    unnamed x23, local copies, waits for them, and re-layouts  8.46 us

profile of v1, /device:TPU:0, one launch (start us, length us, event | category | flops | bytes accessed | tf_op | source)
XLA Modules:
  0.0 105.4 jit_solution(14456236188293405200)
XLA Ops:
  0.0 0.0 copy-start.9
  0.0 0.8 copy.14.halo_count_ref
  0.8 0.7 copy.15.couple_count_ref
  1.5 0.7 copy.16.dw_ref
  2.2 0.0 copy-start
  2.2 1.9 %copy-done = bf16[1,6144,256]{2,1,0:T(8,128)(2,1)S(1)} copy-done((bf16[1,6144,256]{2,1,0:T(8,128)(2,1)S(1)}, bf16[1,6144,256]{2,1,0:T(8,128)(2,1)}, u32[]{:S(2)}) %copy-start) | copy-done | bytes 3145752
  4.1 0.0 copy-start.1
  4.1 0.9 copy-done.1
  5.0 0.0 copy-start.2
  5.0 0.7 copy-done.2
  5.7 0.0 copy-start.3
  5.7 0.7 copy-done.3
  6.4 0.0 copy-start.4
  6.4 0.7 copy-done.4
  7.1 0.0 copy-start.5
  7.1 0.7 copy-done.5
  7.8 0.0 copy-start.6
  7.8 0.7 copy-done.6
  8.5 0.0 copy-start.7
  8.5 0.0 copy-start.8
  8.5 86.0 %couple_and_mix.1 = (bf16[6144,256]{1,0:T(8,128)(2,1)S(1)}, bf16[6144,256]{1,0:T(8,128)(2,1)S(1)}) custom-call(bf16[1,6144,256]{2,1,0:T(8,128)(2,1)S(1)} %copy-done, s32[1,356]{1,0:T(1,128)S(1)} %copy-done.5, s32[1,4,1024]{2,1,0:T(4,128)S(1)} %copy-done.2, s32[1,4,1]{2,1,0:T(4,128)S(1)} %copy.14.halo_count_ref, s32[1,16,128]{2,1,0:T(8,128)S(1)} %copy-done.3, ...), custom_call_target="tpu_custom_call" | custom-call | tf_op jit(solution)/shard_map/couple_and_mix/pallas_call | solution.py:372
  94.4 0.0 copy-done.9
  94.5 0.0 copy-done.7
  94.5 0.0 copy-done.8
  94.5 10.9 %mlp.1 = bf16[1,6144,256]{2,1,0:T(8,128)(2,1)} custom-call(bf16[6144,256]{1,0:T(8,128)(2,1)S(1)} %get-tuple-element.7.normed_ref, bf16[6144,256]{1,0:T(8,128)(2,1)S(1)} %get-tuple-element.8.joined_ref, bf16[1,256,1024]{2,1,0:T(8,128)(2,1)S(1)} %copy-done.7, f32[1,1024]{1,0:T(1,128)S(1)} %copy-done.9, bf16[1,1024,256]{2,1,0:T(8,128)(2,1)S(1)} %copy-done.8), custom_call_target="tpu_custom_call" | custom-call | flops 6442450944 | bytes 9437184 | tf_op jit(solution)/shard_map/mlp/pallas_call | solution.py:420
Async XLA Ops:
  0.0 94.5 %copy-start.9 = (f32[1,1024]{1,0:T(1,128)S(1)}, f32[1,1024]{1,0:T(1,128)}, u32[]{:S(2)}) copy-start(f32[1,1024]{1,0:T(1,128)} %bias_ref.1) | copy-start | bytes 12292
  2.2 1.9 %copy-start = (bf16[1,6144,256]{2,1,0:T(8,128)(2,1)S(1)}, bf16[1,6144,256]{2,1,0:T(8,128)(2,1)}, u32[]{:S(2)}) copy-start(bf16[1,6144,256]{2,1,0:T(8,128)(2,1)} %state_ref.1) | copy-start | bytes 9437188
  4.1 0.9 copy-start.1
  5.0 0.7 copy-start.2
  5.7 0.7 copy-start.3
  6.4 0.7 copy-start.4
  7.1 0.7 copy-start.5
  7.8 0.7 copy-start.6
  8.5 86.0 %copy-start.7 = (bf16[1,256,1024]{2,1,0:T(8,128)(2,1)S(1)}, bf16[1,256,1024]{2,1,0:T(8,128)(2,1)}, u32[]{:S(2)}) copy-start(bf16[1,256,1024]{2,1,0:T(8,128)(2,1)} %up_ref.1) | copy-start | bytes 1572868
  8.5 86.0 %copy-start.8 = (bf16[1,1024,256]{2,1,0:T(8,128)(2,1)S(1)}, bf16[1,1024,256]{2,1,0:T(8,128)(2,1)}, u32[]{:S(2)}) copy-start(bf16[1,1024,256]{2,1,0:T(8,128)(2,1)} %down_ref.1) | copy-start | bytes 1572868

commit v2 on v1

v2 whole, which is shorter than its diff:
```python
import functools

import jax
import jax.numpy as jnp
from jax import lax
from jax.experimental import pallas as pl
from jax.experimental.pallas import tpu as pltpu
from jax.sharding import PartitionSpec as P

MESH = pl.DeviceIdType.MESH
GRID_W = 128
F32 = jnp.float32
BF16 = jnp.bfloat16
TILE = 16


def place(comp, face, tile):
    return {"comp": comp, "face": face, "tile": tile}


def norm(mixed, gain):
    center = mixed - jnp.mean(mixed, axis=-1, keepdims=True)
    spread = jnp.mean(center * center, axis=-1, keepdims=True)
    return center * lax.rsqrt(spread + 1e-06) * gain


def couple_kernel(
    tiles,
    faces,
    cycle_len,
    state_ref,
    cycle_hbm,
    halo_rows_hbm,
    halo_count_hbm,
    couple_rows_hbm,
    couple_count_hbm,
    couple_land_hbm,
    couple_weight_hbm,
    dw_hbm,
    gain_hbm,
    up_hbm,
    bias_hbm,
    down_hbm,
    out_hbm,
    cycle_ref,
    halo_rows_ref,
    halo_count_ref,
    couple_rows_ref,
    couple_count_ref,
    couple_land_ref,
    couple_weight_ref,
    dw_ref,
    gain_ref,
    up_ref,
    bias_ref,
    down_ref,
    rows_bf,
    rows,
    picked,
    send_rows,
    via_rows,
    recv_rows,
    arrived,
    cycle_near,
    index_i32,
    index_smem,
    index_col,
    halo_part,
    halo_send,
    halo_recv,
    border,
    columns,
    normed,
    out,
    load_sem,
    small_sem,
    smem_sem,
    store_sem,
    cross_send_sem,
    cross_recv_sem,
    pass_send_sem,
    pass_recv_sem,
    cycle_send_sem,
    cycle_recv_sem,
    halo_send_sem,
    halo_recv_sem,
):
    comp, face, tile = lax.axis_index("comp"), lax.axis_index("face"), lax.axis_index("tile")
    cells, channels = rows_bf.shape
    half = channels // 2
    height = cells // GRID_W
    slots = couple_rows_ref.shape[2]
    rim_rows = halo_rows_ref.shape[2]
    border_rows = halo_send.shape[1]
    other = 1 - comp
    near = [
        place(comp, face, lax.rem(tile + 1, tiles)),
        place(comp, face, lax.rem(tile + tiles - 1, tiles)),
        place(comp, lax.rem(face + 1, faces), tile),
        place(comp, lax.rem(face + faces - 1, faces), tile),
    ]

    def get_rows(ref, first, count):
        return jnp.concatenate(
            [ref[pl.ds(2 * first + h, count, stride=2), :] for h in range(2)], axis=1
        )

    def put_rows(ref, first, count, value):
        for h in range(2):
            ref[pl.ds(2 * first + h, count, stride=2), :] = value[:, h * half : (h + 1) * half]

    side = 4
    last = tiles - 1

    def distance(k):
        return jnp.where(k == 0, 2, jnp.where(k == side - 1, 0, 2 * k - 1))

    def shifted(n, sign):
        y = lax.rem(tile // side + sign * distance(n // side) + side, side)
        x = lax.rem(lax.rem(tile, side) + sign * distance(lax.rem(n, side)) + side, side)
        return y * side + x

    load_chunks = 4
    chunk = cells // load_chunks

    def load(k):
        part = pl.ds(k * chunk, chunk)
        return pltpu.make_async_copy(state_ref.at[0, part], rows_bf.at[part], load_sem.at[k])

    small = [
        pltpu.make_async_copy(source, target, small_sem.at[q])
        for q, (source, target) in enumerate(
            (
                (couple_rows_hbm, couple_rows_ref),
                (couple_count_hbm, couple_count_ref),
                (cycle_hbm, cycle_ref),
                (halo_rows_hbm, halo_rows_ref),
                (halo_count_hbm, halo_count_ref),
                (couple_land_hbm, couple_land_ref),
                (couple_weight_hbm, couple_weight_ref),
                (dw_hbm, dw_ref),
                (gain_hbm, gain_ref),
                (up_hbm, up_ref),
                (bias_hbm, bias_ref),
                (down_hbm, down_ref),
            )
        )
    ]
    for k in range(load_chunks):
        load(k).start()
    for copy in small:
        copy.start()

    barrier = pltpu.get_barrier_semaphore()

    def greet(n, carry):
        pl.semaphore_signal(
            barrier, inc=1, device_id=place(comp, face, shifted(n, 1)), device_id_type=MESH
        )
        return carry

    lax.fori_loop(0, last, greet, 0)
    for target in (place(other, face, tile), near[2], near[3]):
        pl.semaphore_signal(barrier, inc=1, device_id=target, device_id_type=MESH)

    rows[pl.ds(2 * cells, 16), :] = jnp.zeros((16, half), F32)
    for k in range(load_chunks):
        load(k).wait()

        def widen(i, carry, k=k):
            first = k * chunk + i * 256
            part = pl.ds(pl.multiple_of(first, 256), 256)
            put_rows(rows, first, 256, rows_bf[part, :].astype(F32))
            return carry

        lax.fori_loop(0, chunk // 256, widen, 0)

    for copy in small[:9]:
        copy.wait()
    pl.semaphore_wait(barrier, last + 3)

    def cycle_copy(d):
        return pltpu.make_async_remote_copy(
            src_ref=cycle_ref,
            dst_ref=cycle_near.at[d],
            send_sem=cycle_send_sem.at[d],
            recv_sem=cycle_recv_sem.at[d],
            device_id=near[d ^ 1],
            device_id_type=MESH,
        )

    for d in range(4):
        cycle_copy(d).start()

    def slot_rows(n):
        return pl.ds(pl.multiple_of(n * slots, slots), slots)

    def cross_copy(n):
        own = isinstance(n, int) and n == last
        return pltpu.make_async_remote_copy(
            src_ref=send_rows.at[slot_rows(n)],
            dst_ref=(recv_rows if own else via_rows).at[slot_rows(n)],
            send_sem=cross_send_sem.at[n],
            recv_sem=cross_recv_sem.at[n],
            device_id=place(other, face, tile),
            device_id_type=MESH,
        )

    def pass_copy(n):
        return pltpu.make_async_remote_copy(
            src_ref=via_rows.at[slot_rows(n)],
            dst_ref=recv_rows.at[slot_rows(n)],
            send_sem=pass_send_sem.at[n],
            recv_sem=pass_recv_sem.at[n],
            device_id=place(comp, face, shifted(n, 1)),
            device_id_type=MESH,
        )

    def gather_send(n, carry):
        dest = shifted(n, 1)
        live = couple_count_ref[0, dest]
        step = 64

        def pick(g, inner):
            base = pl.multiple_of(g * step, step)
            index = [
                jnp.where(base + u < live, couple_rows_ref[0, dest, base + u], cells)
                for u in range(step)
            ]
            values = [rows[pl.ds(2 * i, 2), :] for i in index]
            for u in range(step):
                picked[pl.ds(pl.multiple_of(2 * base, 2 * step) + 2 * u, 2), :] = values[u]
            return inner

        lax.fori_loop(0, slots // step, pick, 0)
        send_rows[slot_rows(n), :] = get_rows(picked, 0, slots).astype(BF16)
        cross_copy(n).start()
        return carry

    lax.fori_loop(0, last, gather_send, 0)
    gather_send(last, 0)

    for d in range(4):
        cycle_copy(d).wait()
    index_i32[...] = jnp.full(index_i32.shape, cells, jnp.int32)
    groups = rim_rows // 128
    sub = lax.broadcasted_iota(jnp.int32, (128, cycle_len), 0)
    for d in range(4):
        table = jnp.transpose(
            jnp.concatenate(
                [halo_rows_ref[0, d : d + 1, 128 * g : 128 * (g + 1)] for g in range(groups)], axis=0
            )
        )
        slot = cycle_near[d] - d * rim_rows
        group = jnp.right_shift(slot, 7)
        found = jnp.zeros((128, cycle_len), jnp.int32)
        for g in range(groups):
            found = jnp.where(group == g, table[:, g : g + 1], found)
        found = jnp.where(jnp.bitwise_and(slot, 127) == sub, found, 0)
        found = sum(found[8 * k : 8 * k + 8] for k in range(16))
        row = sum(found[k : k + 1] for k in range(8))
        live = (slot >= 0) & (slot < halo_count_ref[0, d])
        index_i32[d : d + 1, pl.ds(0, cycle_len)] = jnp.where(live, row, cells)
    to_smem = pltpu.make_async_copy(index_i32, index_smem, smem_sem)
    to_smem.start()
    index_col[...] = jnp.transpose(index_i32[...].astype(F32))

    pair = 2 * slots
    pairs = tiles // 2
    early = pairs - 4
    lane_col = lax.broadcasted_iota(jnp.int32, (GRID_W, pair), 0)

    def forward(n):
        cross_copy(n).wait_recv()
        pass_copy(n).start()

    def project(p):
        part = pl.ds(pl.multiple_of(p * pair, pair), pair)
        value = jnp.dot(recv_rows[part, :], couple_weight_ref[0], preferred_element_type=F32)
        arrived[lax.rem(p, 4)] = value.astype(BF16)

    def land_lanes(p):
        return jnp.concatenate(
            [couple_land_ref[0, pl.ds(shifted(2 * p + q, -1), 1), :] for q in range(2)], axis=1
        )

    def landed(p):
        land = land_lanes(p)
        land_row = jnp.right_shift(land, 7)
        in_col = jnp.where(jnp.bitwise_and(land, GRID_W - 1) == lane_col, 1.0, 0.0).astype(BF16)
        hot = jnp.concatenate(
            [in_col * jnp.where(land_row == i, 1.0, 0.0).astype(BF16) for i in range(height)], axis=0
        )
        added = jnp.dot(hot, arrived[lax.rem(p, 4)], preferred_element_type=F32)
        return get_rows(rows, 0, cells) + added

    def land_pair(p):
        pass_copy(2 * p).wait_recv()
        pass_copy(2 * p + 1).wait_recv()
        project(p)
        put_rows(rows, 0, cells, landed(p))

    step = 92

    def pick_halo(d):
        def pick(g, carry):
            values = [
                rows[pl.ds(2 * index_smem[d, g * step + u], 2), :] for u in range(step)
            ]
            start = pl.multiple_of(2 * (d * border_rows + g * step), 2 * step)
            for u in range(step):
                halo_part[pl.ds(start + 2 * u, 2), :] = values[u]
            return carry

        lax.fori_loop(0, border_rows // step, pick, 0)

    forward(0)
    forward(1)

    def early_step(p, carry):
        forward(2 * p)
        forward(2 * p + 1)
        land_pair(p - 1)
        return carry

    lax.fori_loop(1, early + 1, early_step, 0)
    to_smem.wait()

    def pick_step(d, carry):
        pick_halo(d)
        forward(2 * early + 2 + d)
        return carry

    lax.fori_loop(0, 4, pick_step, 0)

    def late_step(p, carry):
        land_pair(p)
        return carry

    lax.fori_loop(early, early + 1, late_step, 0)
    forward(last - 1)
    lax.fori_loop(early + 1, pairs - 1, late_step, 0)
    cross_copy(last).wait_recv()
    pass_copy(last - 1).wait_recv()

    project(pairs - 1)

    def halo_copy(d):
        return pltpu.make_async_remote_copy(
            src_ref=halo_send.at[d],
            dst_ref=halo_recv.at[d],
            send_sem=halo_send_sem.at[d],
            recv_sem=halo_recv_sem.at[d],
            device_id=near[d],
            device_id_type=MESH,
        )

    late_land = jnp.concatenate([land_lanes(p) for p in range(early, pairs)], axis=1).astype(F32)
    late_rows = jnp.concatenate([arrived[p % 4] for p in range(early, pairs)], axis=0)
    for d in (2, 3, 0, 1):
        hot = jnp.where(index_col[pl.ds(0, border_rows), d : d + 1] == late_land, 1.0, 0.0).astype(BF16)
        value = get_rows(halo_part, d * border_rows, border_rows) + jnp.dot(
            hot, late_rows, preferred_element_type=F32
        )
        halo_send[d] = value.astype(BF16)
        halo_copy(d).start()

    joined = landed(pairs - 1).astype(BF16)
    rows_bf[...] = joined
    put_rows(rows, 0, cells, joined.astype(F32))

    taps = [dw_ref[q] for q in range(9)]
    gain = gain_ref[...]

    def mix(above, here, below):
        left, mid, right = (
            taps[c] * above + taps[3 + c] * here + taps[6 + c] * below for c in range(3)
        )
        return mid + pltpu.roll(left, 1, 0) + pltpu.roll(right, GRID_W - 1, 0)

    def grid_row(i):
        return get_rows(rows, i * GRID_W, GRID_W)

    band = 8
    bands = height // band

    def interior(b, carry):
        for q in range(band):
            i = b * band + q
            mixed = mix(
                grid_row(jnp.maximum(i - 1, 0)), grid_row(i), grid_row(jnp.minimum(i + 1, height - 1))
            )
            part = pl.ds(pl.multiple_of(i * GRID_W, GRID_W), GRID_W)
            normed[part, :] = norm(mixed, gain).astype(BF16)
        return carry

    lax.fori_loop(0, bands, interior, 0)

    for copy in small[9:]:
        copy.wait()
    down = (0.5 * down_ref[0].astype(F32)).astype(BF16)

    def mlp(value):
        before = jnp.dot(value, up_ref[0], preferred_element_type=F32) + bias_ref[...]
        return jnp.dot(twice_gelu(before).astype(BF16), down, preferred_element_type=F32)

    def level(first, size):
        part = pl.ds(first, size)
        out[part, :] = (rows_bf[part, :].astype(F32) + mlp(normed[part, :])).astype(BF16)

    def store(k, first, size):
        part = pl.ds(first, size)
        return pltpu.make_async_copy(out.at[part], out_hbm.at[0, part], store_sem.at[k])

    block = 1024
    ahead = 3 * block
    for first in range(0, ahead, block):
        level(first, block)

    outer = ((1, 0), (2, 1), (3, GRID_W - 2), (4, GRID_W - 1))

    for q, col in outer:
        for h in range(2):
            column = rows[pl.ds(2 * col + h, height, stride=2 * GRID_W), :]
            columns[q, pl.ds(1, height), pl.ds(h * half, half)] = column
    for d in range(4):
        halo_copy(d).wait_recv()

    border[...] = (halo_recv[0].astype(F32) + halo_recv[1].astype(F32)) + (
        halo_recv[2].astype(F32) + halo_recv[3].astype(F32)
    )
    wide = GRID_W + 2
    for q, col in outer:
        columns[q, pl.ds(0, 1), :] = border[pl.ds(1 + col, 1), :]
        columns[q, pl.ds(height + 1, 1), :] = border[pl.ds(wide + 1 + col, 1), :]
    for q, corner, side in ((0, 0, 2 * wide), (5, wide - 1, 2 * wide + height)):
        columns[q, pl.ds(0, 1), :] = border[pl.ds(corner, 1), :]
        columns[q, pl.ds(1, height), :] = border[pl.ds(side, height), :]
        columns[q, pl.ds(height + 1, 1), :] = border[pl.ds(wide + corner, 1), :]
    mixed = [
        mix(border[pl.ds(1, GRID_W), :], grid_row(0), grid_row(1)),
        mix(grid_row(height - 2), grid_row(height - 1), border[pl.ds(wide + 1, GRID_W), :]),
    ]
    for first in (0, 3):
        total = None
        for r in range(3):
            for c in range(3):
                term = taps[3 * r + c] * columns[first + c, pl.ds(r, height), :]
                total = term if total is None else total + term
        mixed.append(total)
    edges = norm(jnp.concatenate(mixed, axis=0), gain)
    line = lax.broadcasted_iota(jnp.int32, (TILE, channels), 0)

    def merge(ref, i, left, right):
        for fresh, first, at in ((left, 0, 0), (right, GRID_W - TILE, TILE - 1)):
            box = pl.ds(i * GRID_W + first, TILE)
            fixed = jnp.where(line == at, fresh, ref[box, :].astype(F32))
            ref[box, :] = fixed.astype(BF16)

    lefts, rights = 2 * GRID_W, 2 * GRID_W + height
    normed[pl.ds(cells - GRID_W, GRID_W), :] = edges[GRID_W : 2 * GRID_W].astype(BF16)
    first_row = ahead // GRID_W
    for i in range(first_row, height):
        merge(normed, i, edges[lefts + i : lefts + i + 1], edges[rights + i : rights + i + 1])
    value = jnp.concatenate(
        [edges[:GRID_W], edges[lefts : lefts + first_row], edges[rights : rights + first_row]], axis=0
    )
    around = jnp.concatenate(
        [rows_bf[pl.ds(0, GRID_W), :].astype(F32)]
        + [columns[q, pl.ds(1, first_row), :] for q in (1, 4)],
        axis=0,
    )
    fresh = around + mlp(value.astype(BF16))
    out[pl.ds(0, GRID_W), :] = fresh[:GRID_W].astype(BF16)
    for i in range(first_row):
        left = GRID_W + i
        right = left + first_row
        merge(out, i, fresh[left : left + 1], fresh[right : right + 1])
    stores = [store(0, 0, ahead)]
    stores[0].start()
    for first in range(ahead, cells, block):
        level(first, block)
        stores.append(store(len(stores), first, block))
        stores[-1].start()

    for n in range(tiles):
        cross_copy(n).wait_send()
    for n in range(last):
        pass_copy(n).wait_send()
    for d in range(4):
        halo_copy(d).wait_send()
    for copy in stores:
        copy.wait()


def twice_gelu(before):
    inner = before * (0.7978845608028654 + 0.035677408136300125 * (before * before))
    return before + before * jnp.tanh(inner)


def body(
    state,
    cycle_source,
    halo_rows,
    halo_count,
    couple_rows,
    couple_count,
    couple_land,
    couple_weight,
    dw_weight,
    norm_gain,
    up_weight,
    up_bias,
    down_weight,
):
    _, cells, channels = state.shape
    tiles, faces = lax.axis_size("tile"), lax.axis_size("face")
    cycle_len = cycle_source.shape[1]
    border_rows = -(-cycle_len // TILE) * TILE
    index_lanes = -(-cycle_len // 128) * 128
    slots = couple_rows.shape[2]
    height = cells // GRID_W
    hbm = pl.BlockSpec(memory_space=pl.ANY)
    dma = pltpu.SemaphoreType.DMA
    vmem = pltpu.VMEM
    return pl.pallas_call(
        functools.partial(couple_kernel, tiles, faces, cycle_len),
        name="couple_and_mix",
        out_shape=jax.ShapeDtypeStruct((1, cells, channels), BF16),
        in_specs=[hbm] * 13,
        out_specs=hbm,
        scratch_shapes=[
            vmem((1, cycle_len), jnp.int32),
            vmem(halo_rows.shape, jnp.int32),
            pltpu.SMEM((1, 4), jnp.int32),
            pltpu.SMEM(couple_rows.shape, jnp.int32),
            pltpu.SMEM((1, tiles), jnp.int32),
            vmem(couple_land.shape, jnp.int32),
            vmem(couple_weight.shape, BF16),
            vmem((9, 1, channels), F32),
            vmem((1, channels), F32),
            vmem(up_weight.shape, BF16),
            vmem(up_bias.shape, F32),
            vmem(down_weight.shape, BF16),
            vmem((cells, channels), BF16),
            vmem((2 * cells + 16, channels // 2), F32),
            vmem((2 * slots, channels // 2), F32),
            vmem((tiles * slots, channels), BF16),
            vmem((tiles * slots, channels), BF16),
            vmem((tiles * slots, channels), BF16),
            vmem((4, 2 * slots, channels), BF16),
            vmem((4, 1, cycle_len), jnp.int32),
            vmem((8, index_lanes), jnp.int32),
            pltpu.SMEM((8, index_lanes), jnp.int32),
            vmem((index_lanes, 8), F32),
            vmem((4 * 2 * border_rows, channels // 2), F32),
            vmem((4, border_rows, channels), BF16),
            vmem((4, border_rows, channels), BF16),
            vmem((border_rows, channels), F32),
            vmem((6, height + 8, channels), F32),
            vmem((cells, channels), BF16),
            vmem((cells, channels), BF16),
            dma((4,)),
            dma((12,)),
            dma,
            dma((4,)),
            dma((tiles,)),
            dma((tiles,)),
            dma((tiles,)),
            dma((tiles,)),
            dma((4,)),
            dma((4,)),
            dma((4,)),
            dma((4,)),
        ],
        compiler_params=pltpu.CompilerParams(
            collective_id=0, has_side_effects=True, vmem_limit_bytes=64 << 20
        ),
    )(
        state,
        cycle_source,
        halo_rows,
        halo_count.reshape(1, 4),
        couple_rows,
        couple_count.reshape(1, tiles),
        couple_land,
        couple_weight,
        jnp.transpose(dw_weight, (1, 0, 2)),
        norm_gain,
        up_weight,
        up_bias,
        down_weight,
    )


def solution(mesh):
    in_specs = (
        P("comp", ("face", "tile"), None),
        P("comp", ("face", "tile")),
        P("comp", None, ("face", "tile")),
        P("comp", None, ("face", "tile")),
        P("comp", None, ("face", "tile")),
        P("comp", None, ("face", "tile")),
        P("comp", None, ("face", "tile")),
        P("comp", None, None),
        P("comp", None, None),
        P("comp", None),
        P("comp", None, None),
        P("comp", None),
        P("comp", None, None),
    )
    out_specs = P("comp", ("face", "tile"), None)
    return jax.shard_map(body, mesh=mesh, in_specs=in_specs, out_specs=out_specs, check_vma=False)
```

time: 106 us -> 68.6 us (0.65)
  Pallas kernels: 96.9 us -> 64 us
  local copies, waits for them, and re-layouts: 8.46 us -> 3.76 us
    pallas_call x2 -> x1, Pallas kernels: 96.9 us -> 64 us  [body(): pl.pallas_call(functools.partial(couple_kernel, tiles, faces, cycle_len),...]
    unnamed x23 -> x1, local copies, waits for them, and re-layouts: 8.46 us -> 3.76 us
where the time goes in v2:
time: 68.6 us; the launch traced here: 67.7 us
  Pallas kernels  64 us (93%)
  local copies, waits for them, and re-layouts  3.76 us (5%)
    pallas_call x1, Pallas kernels, body(): pl.pallas_call(functools.partial(couple_kernel, tiles, faces, cycle_len),...  64 us
    unnamed x1, local copies, waits for them, and re-layouts  3.76 us

profile of v2, /device:TPU:0, one launch (start us, length us, event | category | flops | bytes accessed | tf_op | source)
XLA Modules:
  0.0 67.7 jit_solution(8014071849790449105)
XLA Ops:
  0.0 64.0 %couple_and_mix.1 = bf16[1,6144,256]{2,1,0:T(8,128)(2,1)} custom-call(bf16[1,6144,256]{2,1,0:T(8,128)(2,1)} %state_ref.1, s32[1,356]{1,0:T(1,128)} %cycle_hbm.1, s32[1,4,1024]{2,1,0:T(4,128)} %halo_rows_hbm.1, s32[1,4]{1,0:T(1,128)} %bitcast.4, s32[1,16,128]{2,1,0:T(8,128)} %couple_rows_hbm.1, s32[1,16]{1,0:T(1,128)} %bitcast.5, ...), custom_call_target="tpu_custom_call" | custom-call | tf_op jit(solution)/shard_map/couple_and_mix/pallas_call | solution.py:526
  64.0 3.8 %copy.15 = bf16[1,6144,256]{2,1,0:T(8,128)(2,1)} copy(bf16[1,6144,256]{2,1,0:T(8,128)(2,1)} %couple_and_mix.1) | data formatting | bytes 6291456

commit v3 on v2

--- a/solution.py
+++ b/solution.py
@@ -113,7 +113,7 @@
     last = tiles - 1
 
     def distance(k):
-        return jnp.where(k == 0, 2, jnp.where(k == side - 1, 0, 2 * k - 1))
+        return jnp.where(k == 0, 0, jnp.where(k == 1, 3, k - 1))
 
     def shifted(n, sign):
         y = lax.rem(tile // side + sign * distance(n // side) + side, side)
@@ -159,7 +159,7 @@
         )
         return carry
 
-    lax.fori_loop(0, last, greet, 0)
+    lax.fori_loop(1, tiles, greet, 0)
     for target in (place(other, face, tile), near[2], near[3]):
         pl.semaphore_signal(barrier, inc=1, device_id=target, device_id_type=MESH)
 
@@ -195,31 +195,31 @@
     def slot_rows(n):
         return pl.ds(pl.multiple_of(n * slots, slots), slots)
 
-    def cross_copy(n):
-        own = isinstance(n, int) and n == last
+    def pass_copy(n):
         return pltpu.make_async_remote_copy(
             src_ref=send_rows.at[slot_rows(n)],
-            dst_ref=(recv_rows if own else via_rows).at[slot_rows(n)],
+            dst_ref=via_rows.at[slot_rows(n)],
+            send_sem=pass_send_sem.at[n],
+            recv_sem=pass_recv_sem.at[n],
+            device_id=place(comp, face, shifted(n, 1)),
+            device_id_type=MESH,
+        )
+
+    def cross_copy(n):
+        own = isinstance(n, int) and n == 0
+        return pltpu.make_async_remote_copy(
+            src_ref=(send_rows if own else via_rows).at[slot_rows(n)],
+            dst_ref=recv_rows.at[slot_rows(n)],
             send_sem=cross_send_sem.at[n],
             recv_sem=cross_recv_sem.at[n],
             device_id=place(other, face, tile),
             device_id_type=MESH,
         )
 
-    def pass_copy(n):
-        return pltpu.make_async_remote_copy(
-            src_ref=via_rows.at[slot_rows(n)],
-            dst_ref=recv_rows.at[slot_rows(n)],
-            send_sem=pass_send_sem.at[n],
-            recv_sem=pass_recv_sem.at[n],
-            device_id=place(comp, face, shifted(n, 1)),
-            device_id_type=MESH,
-        )
-
-    def gather_send(n, carry):
+    def gather(n):
         dest = shifted(n, 1)
         live = couple_count_ref[0, dest]
-        step = 64
+        step = slots
 
         def pick(g, inner):
             base = pl.multiple_of(g * step, step)
@@ -234,11 +234,15 @@
 
         lax.fori_loop(0, slots // step, pick, 0)
         send_rows[slot_rows(n), :] = get_rows(picked, 0, slots).astype(BF16)
-        cross_copy(n).start()
+
+    def gather_send(n, carry):
+        gather(n)
+        pass_copy(n).start()
         return carry
 
-    lax.fori_loop(0, last, gather_send, 0)
-    gather_send(last, 0)
+    gather(0)
+    cross_copy(0).start()
+    lax.fori_loop(1, tiles, gather_send, 0)
 
     for d in range(4):
         cycle_copy(d).wait()
@@ -263,21 +267,28 @@
         index_i32[d : d + 1, pl.ds(0, cycle_len)] = jnp.where(live, row, cells)
     to_smem = pltpu.make_async_copy(index_i32, index_smem, smem_sem)
     to_smem.start()
-    index_col[...] = jnp.transpose(index_i32[...].astype(F32))
+    turned = jnp.transpose(index_i32[...].astype(F32))
+    for d in range(4):
+        index_col[pl.ds(d * border_rows, border_rows), :] = jnp.broadcast_to(
+            turned[:border_rows, d : d + 1], (border_rows, 128)
+        )
+
+    def forward(n, carry):
+        pass_copy(n).wait_recv()
+        cross_copy(n).start()
+        return carry
+
+    lax.fori_loop(1, tiles, forward, 0)
 
     pair = 2 * slots
     pairs = tiles // 2
-    early = pairs - 4
+    early = pairs - 3
     lane_col = lax.broadcasted_iota(jnp.int32, (GRID_W, pair), 0)
-
-    def forward(n):
-        cross_copy(n).wait_recv()
-        pass_copy(n).start()
 
     def project(p):
         part = pl.ds(pl.multiple_of(p * pair, pair), pair)
         value = jnp.dot(recv_rows[part, :], couple_weight_ref[0], preferred_element_type=F32)
-        arrived[lax.rem(p, 4)] = value.astype(BF16)
+        arrived[p] = value.astype(BF16)
 
     def land_lanes(p):
         return jnp.concatenate(
@@ -291,12 +302,12 @@
         hot = jnp.concatenate(
             [in_col * jnp.where(land_row == i, 1.0, 0.0).astype(BF16) for i in range(height)], axis=0
         )
-        added = jnp.dot(hot, arrived[lax.rem(p, 4)], preferred_element_type=F32)
+        added = jnp.dot(hot, arrived[p], preferred_element_type=F32)
         return get_rows(rows, 0, cells) + added
 
     def land_pair(p):
-        pass_copy(2 * p).wait_recv()
-        pass_copy(2 * p + 1).wait_recv()
+        cross_copy(2 * p).wait_recv()
+        cross_copy(2 * p + 1).wait_recv()
         project(p)
         put_rows(rows, 0, cells, landed(p))
 
@@ -314,34 +325,21 @@
 
         lax.fori_loop(0, border_rows // step, pick, 0)
 
-    forward(0)
-    forward(1)
-
-    def early_step(p, carry):
-        forward(2 * p)
-        forward(2 * p + 1)
-        land_pair(p - 1)
+    def land_step(p, carry):
+        land_pair(p)
         return carry
 
-    lax.fori_loop(1, early + 1, early_step, 0)
+    lax.fori_loop(0, early, land_step, 0)
     to_smem.wait()
 
     def pick_step(d, carry):
         pick_halo(d)
-        forward(2 * early + 2 + d)
         return carry
 
     lax.fori_loop(0, 4, pick_step, 0)
-
-    def late_step(p, carry):
-        land_pair(p)
-        return carry
-
-    lax.fori_loop(early, early + 1, late_step, 0)
-    forward(last - 1)
-    lax.fori_loop(early + 1, pairs - 1, late_step, 0)
+    lax.fori_loop(early, pairs - 1, land_step, 0)
+    cross_copy(last - 1).wait_recv()
     cross_copy(last).wait_recv()
-    pass_copy(last - 1).wait_recv()
 
     project(pairs - 1)
 
@@ -356,14 +354,22 @@
         )
 
     late_land = jnp.concatenate([land_lanes(p) for p in range(early, pairs)], axis=1).astype(F32)
-    late_rows = jnp.concatenate([arrived[p % 4] for p in range(early, pairs)], axis=0)
-    for d in (2, 3, 0, 1):
-        hot = jnp.where(index_col[pl.ds(0, border_rows), d : d + 1] == late_land, 1.0, 0.0).astype(BF16)
-        value = get_rows(halo_part, d * border_rows, border_rows) + jnp.dot(
+    late_rows = jnp.concatenate([arrived[p] for p in range(early, pairs)], axis=0)
+    for d in (2, 0):
+        wanted = index_col[pl.ds(d * border_rows, 2 * border_rows), :]
+        hot = jnp.concatenate(
+            [
+                jnp.where(wanted == late_land[:, 128 * k : 128 * (k + 1)], 1.0, 0.0).astype(BF16)
+                for k in range(late_land.shape[1] // 128)
+            ],
+            axis=1,
+        )
+        value = get_rows(halo_part, d * border_rows, 2 * border_rows) + jnp.dot(
             hot, late_rows, preferred_element_type=F32
         )
-        halo_send[d] = value.astype(BF16)
-        halo_copy(d).start()
+        for q in range(2):
+            halo_send[d + q] = value[q * border_rows : (q + 1) * border_rows].astype(BF16)
+            halo_copy(d + q).start()
 
     joined = landed(pairs - 1).astype(BF16)
     rows_bf[...] = joined
@@ -485,7 +491,7 @@
 
     for n in range(tiles):
         cross_copy(n).wait_send()
-    for n in range(last):
+    for n in range(1, tiles):
         pass_copy(n).wait_send()
     for d in range(4):
         halo_copy(d).wait_send()
@@ -548,11 +554,11 @@
             vmem((tiles * slots, channels), BF16),
             vmem((tiles * slots, channels), BF16),
             vmem((tiles * slots, channels), BF16),
-            vmem((4, 2 * slots, channels), BF16),
+            vmem((tiles // 2, 2 * slots, channels), BF16),
             vmem((4, 1, cycle_len), jnp.int32),
             vmem((8, index_lanes), jnp.int32),
             pltpu.SMEM((8, index_lanes), jnp.int32),
-            vmem((index_lanes, 8), F32),
+            vmem((4 * border_rows, 128), F32),
             vmem((4 * 2 * border_rows, channels // 2), F32),
             vmem((4, border_rows, channels), BF16),
             vmem((4, border_rows, channels), BF16),

time: 68.6 us -> 64 us (0.933); the launches traced: 67.7 us -> 63.8 us
  Pallas kernels: 64 us -> 60.1 us
    pallas_call x1, Pallas kernels: 64 us -> 60.1 us  [body(): pl.pallas_call(functools.partial(couple_kernel, tiles, faces, cycle_len),...]
where the time goes in v3:
time: 64 us; the launch traced here: 63.8 us
  Pallas kernels  60.1 us (94%)
  local copies, waits for them, and re-layouts  3.76 us (6%)
    pallas_call x1, Pallas kernels, body(): pl.pallas_call(functools.partial(couple_kernel, tiles, faces, cycle_len),...  60.1 us
    unnamed x1, local copies, waits for them, and re-layouts  3.76 us

profile of v3, /device:TPU:0, one launch (start us, length us, event | category | flops | bytes accessed | tf_op | source)
XLA Modules:
  0.0 63.8 jit_solution(4799611774789100311)
XLA Ops:
  0.0 60.1 %couple_and_mix.1 = bf16[1,6144,256]{2,1,0:T(8,128)(2,1)} custom-call(bf16[1,6144,256]{2,1,0:T(8,128)(2,1)} %state_ref.1, s32[1,356]{1,0:T(1,128)} %cycle_hbm.1, s32[1,4,1024]{2,1,0:T(4,128)} %halo_rows_hbm.1, s32[1,4]{1,0:T(1,128)} %bitcast.4, s32[1,16,128]{2,1,0:T(8,128)} %couple_rows_hbm.1, s32[1,16]{1,0:T(1,128)} %bitcast.5, ...), custom_call_target="tpu_custom_call" | custom-call | tf_op jit(solution)/shard_map/couple_and_mix/pallas_call | solution.py:532
  60.1 3.8 %copy.15 = bf16[1,6144,256]{2,1,0:T(8,128)(2,1)} copy(bf16[1,6144,256]{2,1,0:T(8,128)(2,1)} %couple_and_mix.1) | data formatting | bytes 6291456

commit v4 on v3

--- a/solution.py
+++ b/solution.py
@@ -55,7 +55,7 @@
     bias_ref,
     down_ref,
     rows_bf,
-    rows,
+    rows_all,
     picked,
     send_rows,
     via_rows,
@@ -100,6 +100,9 @@
         place(comp, lax.rem(face + faces - 1, faces), tile),
     ]
 
+    margin = 16
+    rows = rows_all.at[pl.ds(margin, 2 * cells + margin)]
+
     def get_rows(ref, first, count):
         return jnp.concatenate(
             [ref[pl.ds(2 * first + h, count, stride=2), :] for h in range(2)], axis=1
@@ -148,9 +151,6 @@
     ]
     for k in range(load_chunks):
         load(k).start()
-    for copy in small:
-        copy.start()
-
     barrier = pltpu.get_barrier_semaphore()
 
     def greet(n, carry):
@@ -162,8 +162,11 @@
     lax.fori_loop(1, tiles, greet, 0)
     for target in (place(other, face, tile), near[2], near[3]):
         pl.semaphore_signal(barrier, inc=1, device_id=target, device_id_type=MESH)
-
-    rows[pl.ds(2 * cells, 16), :] = jnp.zeros((16, half), F32)
+    for copy in small:
+        copy.start()
+
+    rows_all[pl.ds(0, margin), :] = jnp.zeros((margin, half), F32)
+    rows_all[pl.ds(2 * cells + margin, margin), :] = jnp.zeros((margin, half), F32)
     for k in range(load_chunks):
         load(k).wait()
 
@@ -278,8 +281,6 @@
         cross_copy(n).start()
         return carry
 
-    lax.fori_loop(1, tiles, forward, 0)
-
     pair = 2 * slots
     pairs = tiles // 2
     early = pairs - 3
@@ -329,7 +330,13 @@
         land_pair(p)
         return carry
 
-    lax.fori_loop(0, early, land_step, 0)
+    def forward_step(p, carry):
+        lax.fori_loop(1 + 5 * p, 6 + 5 * p, forward, 0)
+        land_pair(p)
+        return carry
+
+    lax.fori_loop(0, 3, forward_step, 0)
+    lax.fori_loop(3, early, land_step, 0)
     to_smem.wait()
 
     def pick_step(d, carry):
@@ -387,15 +394,23 @@
     def grid_row(i):
         return get_rows(rows, i * GRID_W, GRID_W)
 
+    def near_row(first):
+        return jnp.concatenate(
+            [rows_all[pl.ds(margin + 2 * first + h, GRID_W, stride=2), :] for h in range(2)], axis=1
+        )
+
     band = 8
     bands = height // band
 
     def interior(b, carry):
         for q in range(band):
             i = b * band + q
-            mixed = mix(
-                grid_row(jnp.maximum(i - 1, 0)), grid_row(i), grid_row(jnp.minimum(i + 1, height - 1))
-            )
+            mixed = None
+            for r in range(3):
+                line = jnp.clip(i + r - 1, 0, height - 1) * GRID_W
+                for c in range(3):
+                    term = taps[3 * r + c] * near_row(line + c - 1)
+                    mixed = term if mixed is None else mixed + term
             part = pl.ds(pl.multiple_of(i * GRID_W, GRID_W), GRID_W)
             normed[part, :] = norm(mixed, gain).astype(BF16)
         return carry
@@ -417,11 +432,6 @@
     def store(k, first, size):
         part = pl.ds(first, size)
         return pltpu.make_async_copy(out.at[part], out_hbm.at[0, part], store_sem.at[k])
-
-    block = 1024
-    ahead = 3 * block
-    for first in range(0, ahead, block):
-        level(first, block)
 
     outer = ((1, 0), (2, 1), (3, GRID_W - 2), (4, GRID_W - 1))
 
@@ -465,26 +475,12 @@
 
     lefts, rights = 2 * GRID_W, 2 * GRID_W + height
     normed[pl.ds(cells - GRID_W, GRID_W), :] = edges[GRID_W : 2 * GRID_W].astype(BF16)
-    first_row = ahead // GRID_W
-    for i in range(first_row, height):
+    normed[pl.ds(0, GRID_W), :] = edges[:GRID_W].astype(BF16)
+    for i in range(height):
         merge(normed, i, edges[lefts + i : lefts + i + 1], edges[rights + i : rights + i + 1])
-    value = jnp.concatenate(
-        [edges[:GRID_W], edges[lefts : lefts + first_row], edges[rights : rights + first_row]], axis=0
-    )
-    around = jnp.concatenate(
-        [rows_bf[pl.ds(0, GRID_W), :].astype(F32)]
-        + [columns[q, pl.ds(1, first_row), :] for q in (1, 4)],
-        axis=0,
-    )
-    fresh = around + mlp(value.astype(BF16))
-    out[pl.ds(0, GRID_W), :] = fresh[:GRID_W].astype(BF16)
-    for i in range(first_row):
-        left = GRID_W + i
-        right = left + first_row
-        merge(out, i, fresh[left : left + 1], fresh[right : right + 1])
-    stores = [store(0, 0, ahead)]
-    stores[0].start()
-    for first in range(ahead, cells, block):
+    block = 1024
+    stores = []
+    for first in range(0, cells, block):
         level(first, block)
         stores.append(store(len(stores), first, block))
         stores[-1].start()
@@ -549,7 +545,7 @@
             vmem(up_bias.shape, F32),
             vmem(down_weight.shape, BF16),
             vmem((cells, channels), BF16),
-            vmem((2 * cells + 16, channels // 2), F32),
+            vmem((2 * cells + 32, channels // 2), F32),
             vmem((2 * slots, channels // 2), F32),
             vmem((tiles * slots, channels), BF16),
             vmem((tiles * slots, channels), BF16),
@@ -569,7 +565,7 @@
             dma((4,)),
             dma((12,)),
             dma,
-            dma((4,)),
+            dma((6,)),
             dma((tiles,)),
             dma((tiles,)),
             dma((tiles,)),

time: 64 us -> 61.8 us (0.966)
  Pallas kernels: 60.1 us -> 57.9 us
    pallas_call x1, Pallas kernels: 60.1 us -> 57.9 us  [body(): pl.pallas_call(functools.partial(couple_kernel, tiles, faces, cycle_len),...]
where the time goes in v4:
time: 61.8 us; the launch traced here: 61.6 us
  Pallas kernels  57.9 us (94%)
  local copies, waits for them, and re-layouts  3.76 us (6%)
    pallas_call x1, Pallas kernels, body(): pl.pallas_call(functools.partial(couple_kernel, tiles, faces, cycle_len),...  57.9 us
    unnamed x1, local copies, waits for them, and re-layouts  3.76 us

profile of v4, /device:TPU:0, one launch (start us, length us, event | category | flops | bytes accessed | tf_op | source)
XLA Modules:
  0.0 61.6 jit_solution(13710910956028033539)
XLA Ops:
  0.0 57.9 %couple_and_mix.1 = bf16[1,6144,256]{2,1,0:T(8,128)(2,1)} custom-call(bf16[1,6144,256]{2,1,0:T(8,128)(2,1)} %state_ref.1, s32[1,356]{1,0:T(1,128)} %cycle_hbm.1, s32[1,4,1024]{2,1,0:T(4,128)} %halo_rows_hbm.1, s32[1,4]{1,0:T(1,128)} %bitcast.4, s32[1,16,128]{2,1,0:T(8,128)} %couple_rows_hbm.1, s32[1,16]{1,0:T(1,128)} %bitcast.5, ...), custom_call_target="tpu_custom_call" | custom-call | tf_op jit(solution)/shard_map/couple_and_mix/pallas_call | solution.py:528
  57.9 3.8 %copy.15 = bf16[1,6144,256]{2,1,0:T(8,128)(2,1)} copy(bf16[1,6144,256]{2,1,0:T(8,128)(2,1)} %couple_and_mix.1) | data formatting | bytes 6291456

commit v5 on v4

--- a/solution.py
+++ b/solution.py
@@ -243,9 +243,16 @@
         pass_copy(n).start()
         return carry
 
+    def forward(n, carry):
+        pass_copy(n).wait_recv()
+        cross_copy(n).start()
+        return carry
+
+    first_batch = 3
     gather(0)
     cross_copy(0).start()
     lax.fori_loop(1, tiles, gather_send, 0)
+    lax.fori_loop(1, 1 + first_batch, forward, 0)
 
     for d in range(4):
         cycle_copy(d).wait()
@@ -276,11 +283,6 @@
             turned[:border_rows, d : d + 1], (border_rows, 128)
         )
 
-    def forward(n, carry):
-        pass_copy(n).wait_recv()
-        cross_copy(n).start()
-        return carry
-
     pair = 2 * slots
     pairs = tiles // 2
     early = pairs - 3
@@ -331,7 +333,8 @@
         return carry
 
     def forward_step(p, carry):
-        lax.fori_loop(1 + 5 * p, 6 + 5 * p, forward, 0)
+        rest = 1 + first_batch + 4 * p
+        lax.fori_loop(rest, rest + 4, forward, 0)
         land_pair(p)
         return carry
 

time: 61.8 us -> 60.3 us (0.976)
  Pallas kernels: 57.9 us -> 56.4 us
    pallas_call x1, Pallas kernels: 57.9 us -> 56.4 us  [body(): pl.pallas_call(functools.partial(couple_kernel, tiles, faces, cycle_len),...]
where the time goes in v5:
time: 60.3 us; the launch traced here: 60.2 us
  Pallas kernels  56.4 us (94%)
  local copies, waits for them, and re-layouts  3.76 us (6%)
    pallas_call x1, Pallas kernels, body(): pl.pallas_call(functools.partial(couple_kernel, tiles, faces, cycle_len),...  56.4 us
    unnamed x1, local copies, waits for them, and re-layouts  3.76 us

profile of v5, /device:TPU:0, one launch (start us, length us, event | category | flops | bytes accessed | tf_op | source)
XLA Modules:
  0.0 60.2 jit_solution(17775997844250586156)
XLA Ops:
  0.0 56.4 %couple_and_mix.1 = bf16[1,6144,256]{2,1,0:T(8,128)(2,1)} custom-call(bf16[1,6144,256]{2,1,0:T(8,128)(2,1)} %state_ref.1, s32[1,356]{1,0:T(1,128)} %cycle_hbm.1, s32[1,4,1024]{2,1,0:T(4,128)} %halo_rows_hbm.1, s32[1,4]{1,0:T(1,128)} %bitcast.4, s32[1,16,128]{2,1,0:T(8,128)} %couple_rows_hbm.1, s32[1,16]{1,0:T(1,128)} %bitcast.5, ...), custom_call_target="tpu_custom_call" | custom-call | tf_op jit(solution)/shard_map/couple_and_mix/pallas_call | solution.py:531
  56.4 3.8 %copy.15 = bf16[1,6144,256]{2,1,0:T(8,128)(2,1)} copy(bf16[1,6144,256]{2,1,0:T(8,128)(2,1)} %couple_and_mix.1) | data formatting | bytes 6291456

commit v6 on v5

--- a/solution.py
+++ b/solution.py
@@ -101,7 +101,7 @@
     ]
 
     margin = 16
-    rows = rows_all.at[pl.ds(margin, 2 * cells + margin)]
+    rows = rows_all.at[pl.ds(margin, 2 * cells + margin + 256)]
 
     def get_rows(ref, first, count):
         return jnp.concatenate(
@@ -548,8 +548,8 @@
             vmem(up_bias.shape, F32),
             vmem(down_weight.shape, BF16),
             vmem((cells, channels), BF16),
-            vmem((2 * cells + 32, channels // 2), F32),
-            vmem((2 * slots, channels // 2), F32),
+            vmem((2 * cells + 288, channels // 2), F32),
+            vmem((2 * slots + 8, channels // 2), F32),
             vmem((tiles * slots, channels), BF16),
             vmem((tiles * slots, channels), BF16),
             vmem((tiles * slots, channels), BF16),
@@ -558,7 +558,7 @@
             vmem((8, index_lanes), jnp.int32),
             pltpu.SMEM((8, index_lanes), jnp.int32),
             vmem((4 * border_rows, 128), F32),
-            vmem((4 * 2 * border_rows, channels // 2), F32),
+            vmem((4 * 2 * border_rows + 8, channels // 2), F32),
             vmem((4, border_rows, channels), BF16),
             vmem((4, border_rows, channels), BF16),
             vmem((border_rows, channels), F32),

time: 60.3 us -> 60.3 us (level)
  no operation moved by 1% of the time
where the time goes in v6:
time: 60.3 us; the launch traced here: 60.2 us
  Pallas kernels  56.4 us (94%)
  local copies, waits for them, and re-layouts  3.76 us (6%)
    pallas_call x1, Pallas kernels, body(): pl.pallas_call(functools.partial(couple_kernel, tiles, faces, cycle_len),...  56.4 us
    unnamed x1, local copies, waits for them, and re-layouts  3.76 us

profile of v6, /device:TPU:0, one launch (start us, length us, event | category | flops | bytes accessed | tf_op | source)
XLA Modules:
  0.0 60.2 jit_solution(11632576736345749915)
XLA Ops:
  0.0 56.4 %couple_and_mix.1 = bf16[1,6144,256]{2,1,0:T(8,128)(2,1)} custom-call(bf16[1,6144,256]{2,1,0:T(8,128)(2,1)} %state_ref.1, s32[1,356]{1,0:T(1,128)} %cycle_hbm.1, s32[1,4,1024]{2,1,0:T(4,128)} %halo_rows_hbm.1, s32[1,4]{1,0:T(1,128)} %bitcast.4, s32[1,16,128]{2,1,0:T(8,128)} %couple_rows_hbm.1, s32[1,16]{1,0:T(1,128)} %bitcast.5, ...), custom_call_target="tpu_custom_call" | custom-call | tf_op jit(solution)/shard_map/couple_and_mix/pallas_call | solution.py:531
  56.4 3.8 %copy.15 = bf16[1,6144,256]{2,1,0:T(8,128)(2,1)} copy(bf16[1,6144,256]{2,1,0:T(8,128)(2,1)} %couple_and_mix.1) | data formatting | bytes 6291456
